TPU v7x, 32 devices: a whole 2x2x4 slice. The times are simulated.
32 devices in a mesh: prow: 16 (over z, y, core), pcol: 2 (over x).
Axes of the slice: x: 2, y: 2, z: 4, core: 2. Of those that a mesh axis runs over, the one named last changes fastest.
Arguments:
- prior_panel: bfloat16 [16384, 12288], P('prow', 'pcol'), may hold values from -0.0546875 to 0.0546875
- prior_solution: bfloat16 [12288, 256], P('pcol', 'prow'), may hold values from -6 to 6
- right_side: bfloat16 [16384, 256], P('prow', 'pcol'), may hold values from -6 to 6
- new_panel: bfloat16 [2, 16384, 512], P(None, 'prow', 'pcol'), may hold values from -0.25 to 0.25
- inverses: bfloat16 [2, 512, 512], P(None, 'pcol'), as said below
Outputs:
- solved: bfloat16 [2, 512, 256], P(None, 'pcol')
- pending: float32 [16384, 256], P('prow', 'pcol')
Inputs may be any that keep to these rules, and one draw needn't show every extreme that they name: `inverses`: each of the two inverse blocks is lower triangular with a positive diagonal.
All inputs are finite; a program needn't handle non-finite values.
Results may differ from a plain program's by a relative error of at most 0.0057.
Values may be sent and summed in bfloat16 or wider, within the bound.
A program may use at most 64 MiB of HBM per device.

v0:
```python
import jax
import jax.numpy as jnp
from jax import lax
from jax.sharding import PartitionSpec as P


def spread(block, axis, owner):
    block = jnp.where(lax.axis_index(axis) == owner, block, jnp.zeros_like(block))
    return lax.psum(block, axis)


def body(prior_panel, prior_solution, right_side, new_panel, inverses):
    local_rows = prior_panel.shape[0]
    block_size = inverses.shape[2]
    pair_rows = 2 * block_size
    partial_value = jnp.dot(
        prior_panel,
        lax.all_gather(prior_solution, "prow", axis=1, tiled=True),
        preferred_element_type=jnp.float32,
    )
    row_ids = lax.axis_index("prow") * local_rows + lax.iota(jnp.int32, local_rows)
    first_panel = jnp.where(
        (row_ids >= block_size)[:, None], new_panel[0], jnp.zeros_like(new_panel[0])
    )
    second_panel = jnp.where(
        (row_ids >= pair_rows)[:, None], new_panel[1], jnp.zeros_like(new_panel[1])
    )
    pending = right_side.astype(jnp.float32) - lax.psum_scatter(
        partial_value, "pcol", scatter_dimension=1, tiled=True
    )
    solved_list = []
    for section, masked in ((0, first_panel), (1, second_panel)):
        diagonal = pending[section * block_size : (section + 1) * block_size].astype(jnp.bfloat16)
        gathered = lax.all_gather(diagonal, "pcol", axis=1, tiled=True)
        result = spread(
            jnp.dot(inverses[section], gathered, preferred_element_type=jnp.float32).astype(
                jnp.bfloat16
            ),
            "prow",
            0,
        )
        update = jnp.dot(masked, result, preferred_element_type=jnp.float32)
        pending = pending - lax.psum_scatter(update, "pcol", scatter_dimension=1, tiled=True)
        solved_list.append(result)
    first_x = solved_list[0]
    second_x = solved_list[1]
    return (jnp.stack([first_x, second_x]), pending)


def solution(mesh):
    return jax.shard_map(
        body,
        mesh=mesh,
        in_specs=(
            P("prow", "pcol"),
            P("pcol", "prow"),
            P("prow", "pcol"),
            P(None, "prow", "pcol"),
            P(None, "pcol", None),
        ),
        out_specs=(P(None, "pcol", None), P("prow", "pcol")),
        check_vma=False,
    )
```

profile of v0, /device:TPU:0, one launch (start us, length us, event | category | flops | bytes accessed | tf_op | source)
XLA Modules:
  0.0 335.1 jit_solution(1964586816087864626)
XLA Ops:
  7.2 0.0 copy-start.1
  7.2 0.0 all-gather.2.cloned.1.call-start
  7.2 0.7 all-gather.2.cloned.1.call-update
  7.9 0.0 reduce-scatter.4.cloned.1.call-start
  8.0 50.2 %all-gather.2.cloned.1.call-done = bf16[6144,256]{0,1:T(8,128)(2,1)} async-done(((bf16[6144,16]{0,1:T(8,128)(2,1)}), bf16[6144,256]{0,1:T(8,128)(2,1)}) %all-gather.2.cloned.1.call-update) | async-done | bytes 3145744 | tf_op jit(solution)/shard_map/all_gather | solution.py:18
  58.2 9.9 %fusion.20 = f32[1024,256]{1,0:T(8,128)} fusion(bf16[1024,6144]{1,0:T(8,128)(2,1)} %param.5, bf16[6144,256]{0,1:T(8,128)(2,1)} %all-gather.2.cloned.1.call-done), kind=kOutput, calls=%fused_computation.29 | convolution fusion | flops 3221225472 | bytes 16777216 | tf_op jit(solution)/shard_map/dot_general | solution.py:16
  68.1 0.0 reduce-scatter.4.cloned.1.call-update
  68.2 0.0 all-reduce.3.cloned.1.call-start
  68.2 19.2 %reduce-scatter.4.cloned.1.call-done = f32[1024,128]{1,0:T(8,128)} async-done(((f32[1024,256]{1,0:T(8,128)}), f32[1024,128]{1,0:T(8,128)}) %reduce-scatter.4.cloned.1.call-update) | async-done | bytes 524304 | tf_op jit(solution)/shard_map/reduce_scatter | solution.py:28
  87.4 1.1 convert_subtract_fusion
  88.5 5.9 %all_gather.10 = bf16[512,256]{1,0:T(8,128)(2,1)S(1)} all-gather(bf16[512,128]{1,0:T(8,128)(2,1)S(1)} %slice.47), channel_id=1, replica_groups=mesh['prow'=16,'pcol'=2] {'pcol'}, dimensions={1}, use_global_device_ids=true | all-gather | bytes 393216 | tf_op jit(solution)/shard_map/all_gather | solution.py:34
  94.5 0.0 copy-done.2
  94.5 0.9 fusion.1
  95.4 0.0 all-reduce.3.cloned.1.call-update
  95.4 0.0 reduce-scatter.6.cloned.1.call-start
  95.5 87.0 %all-reduce.3.cloned.1.call-done = bf16[256,256]{0,1:T(8,128)(2,1)} async-done(((bf16[256,256]{0,1:T(8,128)(2,1)}), bf16[256,256]{0,1:T(8,128)(2,1)}) %all-reduce.3.cloned.1.call-update) | async-done | bytes 131088 | tf_op jit(solution)/shard_map/psum | solution.py:9
  182.6 2.2 fusion.5
  184.8 0.0 reduce-scatter.6.cloned.1.call-update
  184.8 0.0 all-reduce.5.cloned.1.call-start
  184.9 22.0 %reduce-scatter.6.cloned.1.call-done = f32[1024,128]{1,0:T(8,128)} async-done(((f32[1024,256]{1,0:T(8,128)}), f32[1024,128]{1,0:T(8,128)}) %reduce-scatter.6.cloned.1.call-update) | async-done | bytes 524304 | tf_op jit(solution)/shard_map/reduce_scatter | solution.py:43
  206.9 1.1 sub.10
  208.0 6.0 %all_gather.11 = bf16[512,256]{1,0:T(8,128)(2,1)S(1)} all-gather(bf16[512,128]{1,0:T(8,128)(2,1)S(1)} %slice.46), channel_id=1, replica_groups=mesh['prow'=16,'pcol'=2] {'pcol'}, dimensions={1}, use_global_device_ids=true | all-gather | bytes 393216 | tf_op jit(solution)/shard_map/all_gather | solution.py:34
  214.0 0.9 fusion.3
  214.9 0.0 all-reduce.5.cloned.1.call-update
  215.0 0.0 reduce-scatter.8.cloned.1.call-start
  215.0 87.0 %all-reduce.5.cloned.1.call-done = bf16[256,256]{0,1:T(8,128)(2,1)} async-done(((bf16[256,256]{0,1:T(8,128)(2,1)}), bf16[256,256]{0,1:T(8,128)(2,1)}) %all-reduce.5.cloned.1.call-update) | async-done | bytes 131088 | tf_op jit(solution)/shard_map/psum | solution.py:9
  302.0 2.2 fusion.4
  304.3 0.0 reduce-scatter.8.cloned.1.call-update
  304.3 1.0 pad_maximum_fusion
  305.3 0.8 copy.7
  306.1 20.3 %reduce-scatter.8.cloned.1.call-done = f32[1024,128]{1,0:T(8,128)} async-done(((f32[1024,256]{1,0:T(8,128)}), f32[1024,128]{1,0:T(8,128)}) %reduce-scatter.8.cloned.1.call-update) | async-done | bytes 524304 | tf_op jit(solution)/shard_map/reduce_scatter | solution.py:43
  326.4 1.9 sub.11
  (8 shorter events, 0.1 us)
Async XLA Ops:
  7.2 80.3 %copy-start.1 = (bf16[1024,128]{1,0:T(8,128)(2,1)S(1)}, bf16[1024,128]{1,0:T(8,128)(2,1)}, u32[]{:S(2)}) copy-start(bf16[1024,128]{1,0:T(8,128)(2,1)} %param.7) | copy-start | bytes 786436
  7.2 51.0 %all-gather.2.cloned.1.call-start = ((), (), s32[]{:S(2)}) async-start(), calls=%async_computation.3 | async-start | bytes 3342336 | tf_op jit(solution)/shard_map/all_gather | solution.py:18
  7.9 86.6 %copy-start.2 = (bf16[2,256,512]{2,1,0:T(8,128)(2,1)S(1)}, bf16[2,256,512]{2,1,0:T(8,128)(2,1)}, u32[]{:S(2)}) copy-start(bf16[2,256,512]{2,1,0:T(8,128)(2,1)} %param.9) | copy-start | bytes 1572868
  7.9 174.6 %copy-start = (bf16[2,1024,256]{2,1,0:T(8,128)(2,1)S(1)}, bf16[2,1024,256]{2,1,0:T(8,128)(2,1)}, u32[]{:S(2)}) copy-start(bf16[2,1024,256]{2,1,0:T(8,128)(2,1)} %param.8) | copy-start | bytes 3145732
  7.9 79.5 %reduce-scatter.4.cloned.1.call-start = ((), (), s32[]{:S(2)}) async-start(), calls=%async_computation.4 | async-start | bytes 1572864 | tf_op jit(solution)/shard_map/reduce_scatter | solution.py:28
  68.2 114.4 %all-reduce.3.cloned.1.call-start = ((), (), s32[]{:S(2)}) async-start(), calls=%async_computation.5 | async-start | bytes 262144 | tf_op jit(solution)/shard_map/psum | solution.py:9
  95.4 111.5 %reduce-scatter.6.cloned.1.call-start = ((), (), s32[]{:S(2)}) async-start(), calls=%async_computation.6 | async-start | bytes 1572864 | tf_op jit(solution)/shard_map/reduce_scatter | solution.py:43
  184.8 117.2 %all-reduce.5.cloned.1.call-start = ((), (), s32[]{:S(2)}) async-start(), calls=%async_computation.7 | async-start | bytes 262144 | tf_op jit(solution)/shard_map/psum | solution.py:9
  215.0 111.4 %reduce-scatter.8.cloned.1.call-start = ((), (), s32[]{:S(2)}) async-start(), calls=%async_computation.8 | async-start | bytes 1572864 | tf_op jit(solution)/shard_map/reduce_scatter | solution.py:43
Sparse Core Ops, SparseCore 0:
  10.3 47.8 all-gather.1
  68.3 19.1 reduce-scatter.3
  95.6 86.9 all-reduce.2
  184.9 21.9 reduce-scatter.5
  215.1 86.9 all-reduce.4
  304.4 21.9 reduce-scatter.7
where the time goes:
time: 335 us
  waiting for transfers between devices  287 us (86%)
  matrix products  16.2 us (5%)
  between operations  14.2 us (4%)
  blocking collectives  11.9 us (4%)
  other arithmetic  5.08 us (2%)
    psum x2, waiting for transfers between devices, spread(): return lax.psum(block, axis)  174 us
    all_gather x1, waiting for transfers between devices, body(): lax.all_gather(prior_solution, 'prow', axis=1, tiled=True)  50.2 us
    reduce_scatter x2, waiting for transfers between devices, body(): lax.psum_scatter(update, 'pcol', scatter_dimension=1, tiled=True)  42.3 us
    reduce_scatter x1, waiting for transfers between devices, body(): lax.psum_scatter(partial_value, 'pcol', scatter_dimension=1, tiled=True)  19.2 us
    all_gather x2, blocking collectives, body(): gathered = lax.all_gather(diagonal, 'pcol', axis=1, tiled=True)  11.9 us
    dot_general x1, matrix products, body(): jnp.dot(prior_panel, lax.all_gather(prior_solution, 'prow', axis=1, tiled...  9.91 us
  transfers between devices with their start and end apart: 6, of which 6 were waited for; matrix products, arithmetic and copies ran while one was open for 1% of the time, Pallas kernels for 0%

commit v1 on v0

--- a/solution.py
+++ b/solution.py
@@ -6,7 +6,7 @@
 
 def spread(block, axis, owner):
     block = jnp.where(lax.axis_index(axis) == owner, block, jnp.zeros_like(block))
-    return lax.psum(block, axis)
+    return jnp.sum(lax.all_gather(block, axis), axis=0)
 
 
 def body(prior_panel, prior_solution, right_side, new_panel, inverses):

time: 335 us -> 244 us (0.73)
  waiting for transfers between devices: 287 us -> 191 us
  local copies, waits for them, and re-layouts: 0.89 us -> 5.43 us
    psum x2 -> x0, waiting for transfers between devices: 174 us -> none  [spread(): return lax.psum(block, axis)]
    all_gather x0 -> x2, waiting for transfers between devices: none -> 82.6 us  [spread(): return jnp.sum(lax.all_gather(block, axis), axis=0)]
    unnamed x7 -> x9, local copies, waits for them, and re-layouts: 0.85 us -> 5.4 us
    reduce_scatter x2, waiting for transfers between devices: 42.3 us -> 37.8 us  [body(): lax.psum_scatter(update, 'pcol', scatter_dimension=1, tiled=True)]
  transfers between devices with their start and end apart: 6 -> 6, of which waited for: 6 -> 6; matrix products, arithmetic and copies ran while one was open for 1% -> 0% of each run, Pallas kernels for 0% -> 0%
where the time goes in v1:
time: 244 us; the launch traced here: 243 us
  waiting for transfers between devices  191 us (78%)
  matrix products  14.4 us (6%)
  between operations  14.2 us (6%)
  blocking collectives  11.9 us (5%)
  other arithmetic  6.43 us (3%)
  local copies, waits for them, and re-layouts  5.43 us (2%)
    all_gather x2, waiting for transfers between devices, spread(): return jnp.sum(lax.all_gather(block, axis), axis=0)  82.6 us
    all_gather x1, waiting for transfers between devices, body(): lax.all_gather(prior_solution, 'prow', axis=1, tiled=True)  50.2 us
    reduce_scatter x2, waiting for transfers between devices, body(): lax.psum_scatter(update, 'pcol', scatter_dimension=1, tiled=True)  37.8 us
    reduce_scatter x1, waiting for transfers between devices, body(): lax.psum_scatter(partial_value, 'pcol', scatter_dimension=1, tiled=True)  19.2 us
    all_gather x2, blocking collectives, body(): gathered = lax.all_gather(diagonal, 'pcol', axis=1, tiled=True)  11.9 us
    dot_general x1, matrix products, body(): jnp.dot(prior_panel, lax.all_gather(prior_solution, 'prow', axis=1, tiled...  9.91 us
    unnamed x9, local copies, waits for them, and re-layouts  5.4 us
  transfers between devices with their start and end apart: 6, of which 6 were waited for; matrix products, arithmetic and copies ran while one was open for 0% of the time, Pallas kernels for 0%

profile of v1, /device:TPU:0, one launch (start us, length us, event | category | flops | bytes accessed | tf_op | source)
XLA Modules:
  0.0 243.3 jit_solution(13464831863398649971)
XLA Ops:
  7.2 0.0 all-gather.6.cloned.1.call-start
  7.2 0.7 all-gather.6.cloned.1.call-update
  7.9 0.0 reduce-scatter.4.cloned.1.call-start
  8.0 50.2 %all-gather.6.cloned.1.call-done = bf16[6144,256]{0,1:T(8,128)(2,1)} async-done(((bf16[6144,16]{0,1:T(8,128)(2,1)}), bf16[6144,256]{0,1:T(8,128)(2,1)}) %all-gather.6.cloned.1.call-update) | async-done | bytes 3145744 | tf_op jit(solution)/shard_map/all_gather | solution.py:18
  58.2 9.9 %fusion.20 = f32[1024,256]{1,0:T(8,128)} fusion(bf16[1024,6144]{1,0:T(8,128)(2,1)} %param.5, bf16[6144,256]{0,1:T(8,128)(2,1)} %all-gather.6.cloned.1.call-done), kind=kOutput, calls=%fused_computation.31 | convolution fusion | flops 3221225472 | bytes 16777216 | tf_op jit(solution)/shard_map/dot_general | solution.py:16
  68.1 0.0 reduce-scatter.4.cloned.1.call-update
  68.1 0.0 all-gather.8.cloned.1.call-start
  68.2 19.2 %reduce-scatter.4.cloned.1.call-done = f32[1024,128]{1,0:T(8,128)} async-done(((f32[1024,256]{1,0:T(8,128)}), f32[1024,128]{1,0:T(8,128)}) %reduce-scatter.4.cloned.1.call-update) | async-done | bytes 524304 | tf_op jit(solution)/shard_map/reduce_scatter | solution.py:28
  87.4 1.1 convert_subtract_fusion
  88.5 6.0 %all_gather.22 = bf16[512,256]{1,0:T(8,128)(2,1)S(1)} all-gather(bf16[512,128]{1,0:T(8,128)(2,1)S(1)} %slice.47), channel_id=1, replica_groups=mesh['prow'=16,'pcol'=2] {'pcol'}, dimensions={1}, use_global_device_ids=true | all-gather | bytes 393216 | tf_op jit(solution)/shard_map/all_gather | solution.py:34
  94.5 0.9 fusion.1
  95.4 0.0 all-gather.8.cloned.1.call-update
  95.4 0.0 reduce-scatter.6.cloned.1.call-start
  95.5 41.3 %all-gather.8.cloned.1.call-done = bf16[4096,256]{0,1:T(8,128)(2,1)} async-done(((bf16[256,256]{0,1:T(8,128)(2,1)}), bf16[4096,256]{0,1:T(8,128)(2,1)}) %all-gather.8.cloned.1.call-update) | async-done | bytes 2097168 | tf_op jit(solution)/shard_map/all_gather | solution.py:9
  136.8 2.3 copy.8
  139.1 1.2 bitcast_reduce_fusion.1
  140.3 1.3 fusion.5
  141.7 0.0 reduce-scatter.6.cloned.1.call-update
  141.7 0.0 all-gather.10.cloned.1.call-start
  141.7 19.3 %reduce-scatter.6.cloned.1.call-done = f32[1024,128]{1,0:T(8,128)} async-done(((f32[1024,256]{1,0:T(8,128)}), f32[1024,128]{1,0:T(8,128)}) %reduce-scatter.6.cloned.1.call-update) | async-done | bytes 524304 | tf_op jit(solution)/shard_map/reduce_scatter | solution.py:43
  161.1 1.1 sub.10
  162.2 6.0 %all_gather.25 = bf16[512,256]{1,0:T(8,128)(2,1)S(1)} all-gather(bf16[512,128]{1,0:T(8,128)(2,1)S(1)} %slice.46), channel_id=1, replica_groups=mesh['prow'=16,'pcol'=2] {'pcol'}, dimensions={1}, use_global_device_ids=true | all-gather | bytes 393216 | tf_op jit(solution)/shard_map/all_gather | solution.py:34
  168.1 0.9 fusion.3
  169.1 0.0 all-gather.10.cloned.1.call-update
  169.1 0.0 reduce-scatter.8.cloned.1.call-start
  169.2 41.3 %all-gather.10.cloned.1.call-done = bf16[4096,256]{0,1:T(8,128)(2,1)} async-done(((bf16[256,256]{0,1:T(8,128)(2,1)}), bf16[4096,256]{0,1:T(8,128)(2,1)}) %all-gather.10.cloned.1.call-update) | async-done | bytes 2097168 | tf_op jit(solution)/shard_map/all_gather | solution.py:9
  210.5 2.2 copy.9
  212.7 1.2 bitcast_reduce_fusion
  213.9 1.3 fusion.4
  215.3 0.8 copy.7
  216.1 18.5 %reduce-scatter.8.cloned.1.call-done = f32[1024,128]{1,0:T(8,128)} async-done(((f32[1024,256]{1,0:T(8,128)}), f32[1024,128]{1,0:T(8,128)}) %reduce-scatter.8.cloned.1.call-update) | async-done | bytes 524304 | tf_op jit(solution)/shard_map/reduce_scatter | solution.py:43
  234.6 1.9 sub.11
  (12 shorter events, 0.1 us)
Async XLA Ops:
  7.2 51.0 %all-gather.6.cloned.1.call-start = ((), (), s32[]{:S(2)}) async-start(), calls=%async_computation.3 | async-start | bytes 3342336 | tf_op jit(solution)/shard_map/all_gather | solution.py:18
  7.9 79.5 %copy-start.1 = (bf16[1024,128]{1,0:T(8,128)(2,1)S(1)}, bf16[1024,128]{1,0:T(8,128)(2,1)}, u32[]{:S(2)}) copy-start(bf16[1024,128]{1,0:T(8,128)(2,1)} %param.7) | copy-start | bytes 786436
  7.9 86.6 %copy-start.2 = (bf16[2,256,512]{2,1,0:T(8,128)(2,1)S(1)}, bf16[2,256,512]{2,1,0:T(8,128)(2,1)}, u32[]{:S(2)}) copy-start(bf16[2,256,512]{2,1,0:T(8,128)(2,1)} %param.9) | copy-start | bytes 1572868
  7.9 79.5 %reduce-scatter.4.cloned.1.call-start = ((), (), s32[]{:S(2)}) async-start(), calls=%async_computation.4 | async-start | bytes 1572864 | tf_op jit(solution)/shard_map/reduce_scatter | solution.py:28
  68.1 68.7 %all-gather.8.cloned.1.call-start = ((), (), s32[]{:S(2)}) async-start(), calls=%async_computation.7 | async-start | bytes 2228224 | tf_op jit(solution)/shard_map/all_gather | solution.py:9
  95.4 65.6 %reduce-scatter.6.cloned.1.call-start = ((), (), s32[]{:S(2)}) async-start(), calls=%async_computation.5 | async-start | bytes 1572864 | tf_op jit(solution)/shard_map/reduce_scatter | solution.py:43
  136.8 3.5 %copy-start = (bf16[2,1024,256]{2,1,0:T(8,128)(2,1)S(1)}, bf16[2,1024,256]{2,1,0:T(8,128)(2,1)}, u32[]{:S(2)}) copy-start(bf16[2,1024,256]{2,1,0:T(8,128)(2,1)} %param.8) | copy-start | bytes 3145732
  141.7 68.8 %all-gather.10.cloned.1.call-start = ((), (), s32[]{:S(2)}) async-start(), calls=%async_computation.8 | async-start | bytes 2228224 | tf_op jit(solution)/shard_map/all_gather | solution.py:9
  169.1 65.5 %reduce-scatter.8.cloned.1.call-start = ((), (), s32[]{:S(2)}) async-start(), calls=%async_computation.6 | async-start | bytes 1572864 | tf_op jit(solution)/shard_map/reduce_scatter | solution.py:43
Sparse Core Ops, SparseCore 0:
  10.3 47.8 all-gather.5
  68.3 19.1 reduce-scatter.3
  95.6 41.1 all-gather.7
  141.8 19.2 reduce-scatter.5
  169.2 41.1 all-gather.9
  215.3 19.2 reduce-scatter.7
